TPU v7x, 128 devices: a whole 4x4x4 slice. The times are simulated.
128 devices in a mesh: gx: 4 (over x_lo, core), gy: 4 (over z), gz: 8 (over y, x_hi).
Axes of the slice: x: 4 (x_hi: 2, x_lo: 2; x = x_hi * 2 + x_lo), y: 4, z: 4, core: 2. Of those that a mesh axis runs over, the one named last changes fastest.
Arguments:
- volume: float32 [128, 512, 1024], P('gx', 'gy', 'gz'), may hold values from -6 to 6
- offsets: int32 [4, 3], replicated, may hold values from -3 to 3, as said below
Outputs:
- denoised: float32 [128, 512, 1024], P('gx', 'gy', 'gz')
Inputs may be any that keep to these rules, and one draw needn't show every extreme that they name: Four distinct offsets; in each the first nonzero component is positive. One offset has first component 3 and a negative third component, another has second component -3, one lies in the plane of the last two dimensions with positive second component, and one lies along the third dimension only; their order is random.
All inputs are finite; a program needn't handle non-finite values.
Results may differ from a plain program's by a relative error of at most 0.00002.
Values sent between devices are 32-bit elements; how exact they have to be, the bound alone decides.
A program may use at most 128 MiB of HBM per device.

v0:
```python
import functools
import math

import jax
import jax.numpy as jnp
from jax import lax
from jax.experimental import pallas as pl
from jax.experimental.pallas import tpu as pltpu
from jax.sharding import PartitionSpec as P

SX, SY, SZ = 32, 128, 128
PAIRS = 4
KAPPA = math.sqrt(math.log2(math.e) / 54.0)
BIG = 16384.0
GROUPS = 9
BLOCK = 5
F32 = jnp.float32
BF16 = jnp.bfloat16
MESH = pl.DeviceIdType.MESH

SIDES = [(dx, dy) for dx in (-1, 0, 1) for dy in (-1, 0, 1) if (dx, dy) != (0, 0)]


def iota(shape, dim):
    return lax.broadcasted_iota(jnp.int32, shape, dim)


def kernel(counts, off, v, out, ext, sh, own, pk_out, pk_in, qh, q2, ql, qr, re, de, eh, el, band, xs, carry, w1, w2,
           send_sem, recv_sem, zsend, zrecv, own_sem):
    nx, ny, nz = counts
    gx, gy, gz = lax.axis_index("gx"), lax.axis_index("gy"), lax.axis_index("gz")

    def have(dx, dy, dz):
        ok = True
        for at, d, n in ((gx, dx, nx), (gy, dy, ny), (gz, dz, nz)):
            if d > 0:
                ok = jnp.logical_and(ok, at + d < n)
            elif d < 0:
                ok = jnp.logical_and(ok, at + d >= 0)
        return ok

    mine = pltpu.make_async_copy(v, ext.at[4:36, 8:136, :], own_sem)
    mine.start()

    barrier = pltpu.get_barrier_semaphore()
    total = jnp.int32(0)
    for dx, dy, dz in [(dx, dy, 0) for dx, dy in SIDES] + [(0, 0, -1), (0, 0, 1)]:
        ok = have(dx, dy, dz)
        total = total + ok.astype(jnp.int32)

        @pl.when(ok)
        def _():
            pl.semaphore_signal(barrier, inc=1, device_id={"gx": gx + dx, "gy": gy + dy, "gz": gz + dz}, device_id_type=MESH)

    pl.semaphore_wait(barrier, total)

    src_x = {1: pl.ds(28, 4), -1: pl.ds(0, 4), 0: pl.ds(0, 32)}
    dst_x = {1: pl.ds(0, 4), -1: pl.ds(36, 4), 0: pl.ds(4, 32)}
    src_y = {1: pl.ds(120, 8), -1: pl.ds(0, 8), 0: pl.ds(0, 128)}
    dst_y = {1: pl.ds(0, 8), -1: pl.ds(136, 8), 0: pl.ds(8, 128)}

    def side_copy(i):
        dx, dy = SIDES[i]
        return pltpu.make_async_remote_copy(
            src_ref=v.at[src_x[dx], src_y[dy], :],
            dst_ref=ext.at[dst_x[dx], dst_y[dy], :],
            send_sem=send_sem.at[i],
            recv_sem=recv_sem.at[i],
            device_id={"gx": gx + dx, "gy": gy + dy},
            device_id_type=MESH,
        )

    for i, (dx, dy) in enumerate(SIDES):

        @pl.when(have(dx, dy, 0))
        def _():
            side_copy(i).start()

        @pl.when(jnp.logical_not(have(-dx, -dy, 0)))
        def _():
            shape = (4 if dx else 32, 8 if dy else 128, 128)
            ext[dst_x[dx], dst_y[dy], :] = jnp.zeros(shape, F32)

    mine.wait()
    for i, (dx, dy) in enumerate(SIDES):

        @pl.when(have(-dx, -dy, 0))
        def _():
            side_copy(i).wait_recv()

    lane = iota((16, 128), 1)
    group = iota((16, 128), 0)
    slot = lane % 8
    low = slot < 4

    def pack_plane(x, _):
        lane8 = iota((8, 128), 1)
        acc = jnp.zeros((8, 128), F32)
        last = jnp.zeros((8, 128), F32)
        for j in range(16):
            here = lane8 // 8 == 15 - j
            turn = (4 + 8 * (15 - j)) % 128
            acc = jnp.where(here, pltpu.roll(ext[x, pl.ds(4 + j, 8, stride=16), :], turn, axis=1), acc)
            if j < 8:
                rows = jnp.broadcast_to(ext[x, pl.ds(132 + j, 1), :], (8, 128))
                last = jnp.where(here, pltpu.roll(rows, turn, axis=1), last)
        own[x, 0:8, :] = acc
        own[x, 8:16, :] = jnp.where(iota((8, 128), 0) == 0, last, 0.0)
        return 0

    lax.fori_loop(0, 40, pack_plane, 0)

    def pack_pair(x, _):
        near, far = own[x], own[x + 20]
        pk_out[0, x] = jnp.where(low, near, pltpu.roll(far, 4, axis=1))
        pk_out[1, x] = jnp.where(low, pltpu.roll(near, 124, axis=1), far)
        return 0

    lax.fori_loop(0, 20, pack_pair, 0)

    def z_copy(i):
        return pltpu.make_async_remote_copy(
            src_ref=pk_out.at[i],
            dst_ref=pk_in.at[i],
            send_sem=zsend.at[i],
            recv_sem=zrecv.at[i],
            device_id={"gz": gz + (1 - 2 * i)},
            device_id_type=MESH,
        )

    for i in range(2):
        d = 1 - 2 * i

        @pl.when(have(0, 0, d))
        def _():
            z_copy(i).start()

        @pl.when(jnp.logical_not(have(0, 0, -d)))
        def _():
            pk_in[i] = jnp.zeros((20, 16, 128), F32)

    def make_band(k, _):
        c = off[k, 2]
        row, col = iota((128, 256), 0), iota((128, 256), 1)
        fwd = col < 128
        spot = jnp.where(fwd, col, col - 128 - c)
        hit = jnp.where(jnp.abs(row - spot) <= 1, -1.0, 0.0)
        s = row % 8
        edge_z = jnp.where(s < 4, s - 4, s + 124)
        edge = jnp.where(jnp.abs(edge_z - spot) <= 1, -1.0, 0.0)
        first = jnp.where(c > 0, 5, 0)
        at = gz * SZ + jnp.where(fwd, col + c, spot)
        beyond = jnp.logical_or(at < 0, at >= nz * SZ)
        edge = jnp.where(s == first, jnp.where(fwd, -BIG, 0.0), edge)
        edge = jnp.where(s == first + 1, jnp.where(fwd, 0.0, -BIG), edge)
        edge = jnp.where(s == first + 2, jnp.where(beyond, -BIG, 0.0), edge)
        hit, edge = hit.astype(BF16), edge.astype(BF16)
        band[k, 0:128, :] = hit
        band[k, 128:256, :] = hit
        band[k, 256:384, :] = edge
        band[k, 384:512, :] = edge
        return 0

    lax.fori_loop(0, PAIRS, make_band, 0)
    xs[...] = jnp.zeros_like(xs)
    re[...] = jnp.zeros_like(re)

    for i in range(2):
        d = 1 - 2 * i

        @pl.when(have(0, 0, -d))
        def _():
            z_copy(i).wait_recv()

    def unpack(x, _):
        left, right = pk_in[0, x], pk_in[1, x]
        for at, from_left, from_right in (
            (x, left, pltpu.roll(right, 4, axis=1)),
            (x + 20, pltpu.roll(left, 124, axis=1), right),
        ):
            mid = own[at]
            halo = jnp.where(low, from_left, from_right) * KAPPA
            qh[at] = halo
            q2[at] = pltpu.roll(halo, 64, axis=1)
            ql[at] = jnp.where(low, from_left, mid) * KAPPA
            qr[at] = jnp.where(low, mid, from_right) * KAPPA
        return 0

    lax.fori_loop(0, 20, unpack, 0)

    def shift_plane(x, _):
        for t in range(18):
            lane8 = iota((8, 128), 1)
            val = ext[x, 8 * t : 8 * t + 8, :] * KAPPA
            halves = []
            if t > 0:
                r0 = 8 * t - 4
                g0, j0 = r0 // 16, r0 % 16
            else:
                g0, j0 = 0, -4
            source = q2 if j0 >= 8 or j0 < 0 else qh
            a = jnp.broadcast_to(source[x, pl.ds(g0, 1), :], (8, 128))
            if j0 + 7 >= 16:
                b = jnp.broadcast_to(source[x, pl.ds(g0 + 1, 1), :], (8, 128))
                a = jnp.where(iota((8, 128), 0) + j0 >= 16, b, a)
            halo = pltpu.roll(a, (8 * (j0 % 8) + 4) % 128, axis=1, stride=8, stride_axis=0)
            sh[3, x, 8 * t : 8 * t + 8, :] = val
            for s in (1, 2, 3):
                sh[3 + s, x, 8 * t : 8 * t + 8, :] = pltpu.roll(jnp.where(lane8 < s, halo, val), 128 - s, axis=1)
                sh[3 - s, x, 8 * t : 8 * t + 8, :] = pltpu.roll(jnp.where(lane8 >= 128 - s, halo, val), s, axis=1)
        return 0

    lax.fori_loop(0, 40, shift_plane, 0)

    def edges(k, _):
        a, b, c = off[k, 0], off[k, 1], off[k, 2]
        turn = lax.rem(128 + 8 * b - c, 128)
        step = jnp.where(b < 0, -1, 1)

        def turned(x, _):
            left = pltpu.roll(ql[x], turn, axis=1)
            right = pltpu.roll(qr[x], turn, axis=1)
            re[x, 8:24, :] = jnp.where(low, left, right)
            return 0

        lax.fori_loop(0, 40, turned, 0)
        row = 15 - lane // 8 + b
        inner = jnp.logical_and(row >= 0, row < 16)

        def squares(x, _):
            same = re[x + a, 8:24, :]
            other = re[x + a, pl.ds(8 + step, 16), :]
            diff = qh[x] - jnp.where(inner, same, other)
            de[x] = diff * diff
            return 0

        lax.fori_loop(0, 37, squares, 0)

        first = jnp.where(c > 0, 5, 0)
        y_at = gy * SY + 16 * group + 15 - lane // 8 - 4
        y_to = y_at + b
        one, zero = jnp.float32(1.0), jnp.float32(0.0)
        out_to = jnp.where(jnp.logical_or(y_to < 0, y_to >= ny * SY), one, zero)
        out_at = jnp.where(jnp.logical_or(y_at < 0, y_at >= ny * SY), one, zero)
        flag_y = jnp.where(slot == first, out_to, jnp.where(slot == first + 1, out_at, one))
        is_flag = jnp.logical_and(slot >= first, slot < first + 3)

        def sums(p, _):
            field = de[p] + de[p + 1] + de[p + 2]
            up = pltpu.roll(field, 8, axis=1)
            up = jnp.where(lane >= 8, up, pltpu.roll(up, 15, axis=0))
            down = pltpu.roll(field, 120, axis=1)
            down = jnp.where(lane < 120, down, pltpu.roll(down, 1, axis=0))
            field = field + up + down
            x_at = gx * SX + p - 3
            x_to = x_at + a
            fx_to = jnp.where(jnp.logical_or(x_to < 0, x_to >= nx * SX), one, zero)
            fx_at = jnp.where(jnp.logical_or(x_at < 0, x_at >= nx * SX), one, zero)
            flag_x = jnp.where(slot == first, fx_to, jnp.where(slot == first + 1, fx_at, zero))
            field = jnp.where(is_flag, jnp.maximum(flag_x, flag_y), field)
            high = field.astype(BF16).astype(F32)
            eh[k, p] = high
            el[k, p] = field - high
            return 0

        lax.fori_loop(0, 35, sums, 0)
        return 0

    lax.fori_loop(0, PAIRS, edges, 0)

    diag = iota((16, 128), 1) // 8 == 15 - iota((16, 128), 0)

    def pair(k, _):
        a, b, c = off[k, 0], off[k, 1], off[k, 2]

        def square(x, t):
            diff = sh[3, x, pl.ds(8 * t + 4, 8), :] - sh[3 + c, x + a, pl.ds(8 * t + 4 + b, 8), :]
            return diff * diff

        for t in range(17):
            d0, d1 = square(0, t), square(1, t)
            carry[0, 8 * t : 8 * t + 8, :] = d0 + d1
            carry[1, 8 * t : 8 * t + 8, :] = d1

        def block(n, _):
            p = n * BLOCK
            for t in range(17):
                rows = slice(8 * t, 8 * t + 8)
                d = [square(p + 2 + i, t) for i in range(5)]
                d01 = d[0] + d[1]
                d23 = d[2] + d[3]
                xs[0, 8 + 8 * t : 16 + 8 * t, :] = carry[0, rows, :] + d[0]
                xs[1, 8 + 8 * t : 16 + 8 * t, :] = carry[1, rows, :] + d01
                xs[2, 8 + 8 * t : 16 + 8 * t, :] = d01 + d[2]
                xs[3, 8 + 8 * t : 16 + 8 * t, :] = d[1] + d23
                xs[4, 8 + 8 * t : 16 + 8 * t, :] = d23 + d[4]
                carry[0, rows, :] = d[3] + d[4]
                carry[1, rows, :] = d[4]
            for i in range(BLOCK):
                left = []
                for g in range(GROUPS):
                    r = 8 + 16 * g
                    field = xs[i, r - 1 : r + 15, :] + xs[i, r : r + 16, :] + xs[i, r + 1 : r + 17, :]
                    high = field.astype(BF16)
                    rest = (field - high.astype(F32)).astype(BF16)
                    e_high = jnp.broadcast_to(eh[k, p + i, pl.ds(g, 1), :], (16, 128)).astype(BF16)
                    e_rest = jnp.broadcast_to(el[k, p + i, pl.ds(g, 1), :], (16, 128)).astype(BF16)
                    zero = jnp.zeros((), BF16)
                    left.append(
                        jnp.concatenate(
                            [high, rest, jnp.where(diag, e_high, zero), jnp.where(diag, e_rest, zero)], axis=1
                        )
                    )
                left = jnp.concatenate(left, axis=0)
                weight = jnp.exp2(jnp.dot(left, band[k], preferred_element_type=F32))
                w1[k, p + i] = weight[0:136, 0:128]
                w2[k, p + i] = weight[0:136, 128:256]
            return 0

        lax.fori_loop(0, 7, block, 0)
        return 0

    lax.fori_loop(0, PAIRS, pair, 0)

    def finish(x, _):
        for t in range(16):
            y = 8 * t
            num = sh[3, x + 4, y + 8 : y + 16, :]
            den = jnp.ones((8, 128), F32)
            for k in range(PAIRS):
                a, b, c = off[k, 0], off[k, 1], off[k, 2]
                near = sh[3 + c, x + 4 + a, pl.ds(y + 8 + b, 8), :]
                back = sh[3 - c, x + 4 - a, pl.ds(y + 8 - b, 8), :]
                fore_w = w1[k, x + 3, y + 4 : y + 12, :]
                back_w = w2[k, x + 3 - a, pl.ds(y + 4 - b, 8), :]
                num = num + fore_w * near + back_w * back
                den = den + fore_w + back_w
            out[x, y : y + 8, :] = num / (den * KAPPA)
        return 0

    lax.fori_loop(0, SX, finish, 0)

    for i, (dx, dy) in enumerate(SIDES):

        @pl.when(have(dx, dy, 0))
        def _():
            side_copy(i).wait_send()

    for i in range(2):

        @pl.when(have(0, 0, 1 - 2 * i))
        def _():
            z_copy(i).wait_send()


def local(counts, volume, offsets):
    return pl.pallas_call(
        functools.partial(kernel, counts),
        out_shape=jax.ShapeDtypeStruct((SX, SY, SZ), F32),
        in_specs=[pl.BlockSpec(memory_space=pltpu.SMEM), pl.BlockSpec(memory_space=pl.ANY)],
        out_specs=pl.BlockSpec(memory_space=pltpu.VMEM),
        scratch_shapes=[
            pltpu.VMEM((40, 144, 128), F32),
            pltpu.VMEM((7, 40, 144, 128), F32),
            pltpu.VMEM((40, 16, 128), F32),
            pltpu.VMEM((2, 20, 16, 128), F32),
            pltpu.VMEM((2, 20, 16, 128), F32),
            pltpu.VMEM((40, 16, 128), F32),
            pltpu.VMEM((40, 16, 128), F32),
            pltpu.VMEM((40, 16, 128), F32),
            pltpu.VMEM((40, 16, 128), F32),
            pltpu.VMEM((40, 32, 128), F32),
            pltpu.VMEM((37, 16, 128), F32),
            pltpu.VMEM((PAIRS, 35, 16, 128), F32),
            pltpu.VMEM((PAIRS, 35, 16, 128), F32),
            pltpu.VMEM((PAIRS, 512, 256), BF16),
            pltpu.VMEM((BLOCK, 168, 128), F32),
            pltpu.VMEM((2, 136, 128), F32),
            pltpu.VMEM((PAIRS, 35, 136, 128), F32),
            pltpu.VMEM((PAIRS, 35, 136, 128), F32),
            pltpu.SemaphoreType.DMA((8,)),
            pltpu.SemaphoreType.DMA((8,)),
            pltpu.SemaphoreType.DMA((2,)),
            pltpu.SemaphoreType.DMA((2,)),
            pltpu.SemaphoreType.DMA,
        ],
        compiler_params=pltpu.CompilerParams(
            collective_id=0, has_side_effects=True, vmem_limit_bytes=62 * 1024 * 1024
        ),
    )(offsets, volume)


def solution(mesh):
    counts = (mesh.shape["gx"], mesh.shape["gy"], mesh.shape["gz"])
    spec = P("gx", "gy", "gz")
    return jax.shard_map(
        functools.partial(local, counts), mesh=mesh, in_specs=(spec, P()), out_specs=spec, check_vma=False
    )
```

profile of v0, /device:TPU:1, one launch (start us, length us, event | category | flops | bytes accessed | tf_op | source)
XLA Modules:
  0.0 86.8 jit_solution(11851601325303366967)
XLA Ops:
  0.0 83.6 %shard_map.28 = f32[32,128,128]{2,1,0:T(8,128)} custom-call(s32[4,3]{1,0:T(4,128)} %off.1, f32[32,128,128]{2,1,0:T(8,128)} %v.1), custom_call_target="tpu_custom_call" | custom-call | tf_op jit(solution)/shard_map/pallas_call | solution.py:357
  83.7 3.1 %copy.4 = f32[32,128,128]{2,1,0:T(8,128)} copy(f32[32,128,128]{2,1,0:T(8,128)} %shard_map.28) | data formatting | bytes 4194304
where the time goes:
time: 86.9 us; the launch traced here: 86.8 us
  Pallas kernels  83.6 us (96%)
  local copies, waits for them, and re-layouts  3.14 us (4%)
    pallas_call x1, Pallas kernels, local(): pl.pallas_call(functools.partial(kernel, counts), out_shape=jax.ShapeDtyp...  83.6 us
    unnamed x1, local copies, waits for them, and re-layouts  3.14 us

commit v1 on v0

v1 whole, which is shorter than its diff:
```python
import functools
import math

import jax
import jax.numpy as jnp
from jax import lax
from jax.experimental import pallas as pl
from jax.experimental.pallas import tpu as pltpu
from jax.sharding import PartitionSpec as P

SX, SY, SZ = 32, 128, 128
PAIRS = 4
KAPPA = math.sqrt(math.log2(math.e) / 54.0)
BIG = 16384.0
GROUPS = 9
BLOCK = 6
STEPS = 6
TOGETHER = 2
F32 = jnp.float32
BF16 = jnp.bfloat16
MESH = pl.DeviceIdType.MESH

SIDES = [(dx, dy) for dx in (-1, 0, 1) for dy in (-1, 0, 1) if (dx, dy) != (0, 0)]


def iota(shape, dim):
    return lax.broadcasted_iota(jnp.int32, shape, dim)


def kernel(counts, off, v, out, ext, sv, hal, near, own, pk_out, pk_in, qh, ql, qr, re, de, fs, eh, el, band, xa, xb, carry, w1, w2,
           send_sem, recv_sem, zsend, zrecv, own_sem):
    nx, ny, nz = counts
    gx, gy, gz = lax.axis_index("gx"), lax.axis_index("gy"), lax.axis_index("gz")

    def have(dx, dy, dz):
        ok = True
        for at, d, n in ((gx, dx, nx), (gy, dy, ny), (gz, dz, nz)):
            if d > 0:
                ok = jnp.logical_and(ok, at + d < n)
            elif d < 0:
                ok = jnp.logical_and(ok, at + d >= 0)
        return ok

    mine = pltpu.make_async_copy(v, ext.at[4:36, 8:136, :], own_sem)
    mine.start()

    barrier = pltpu.get_barrier_semaphore()
    total = jnp.int32(0)
    for dx, dy, dz in [(dx, dy, 0) for dx, dy in SIDES] + [(0, 0, -1), (0, 0, 1)]:
        ok = have(dx, dy, dz)
        total = total + ok.astype(jnp.int32)

        @pl.when(ok)
        def _():
            pl.semaphore_signal(barrier, inc=1, device_id={"gx": gx + dx, "gy": gy + dy, "gz": gz + dz}, device_id_type=MESH)

    pl.semaphore_wait(barrier, total)

    src_x = {1: pl.ds(28, 4), -1: pl.ds(0, 4), 0: pl.ds(0, 32)}
    dst_x = {1: pl.ds(0, 4), -1: pl.ds(36, 4), 0: pl.ds(4, 32)}
    src_y = {1: pl.ds(120, 8), -1: pl.ds(0, 8), 0: pl.ds(0, 128)}
    dst_y = {1: pl.ds(0, 8), -1: pl.ds(136, 8), 0: pl.ds(8, 128)}

    def side_copy(i):
        dx, dy = SIDES[i]
        return pltpu.make_async_remote_copy(
            src_ref=v.at[src_x[dx], src_y[dy], :],
            dst_ref=ext.at[dst_x[dx], dst_y[dy], :],
            send_sem=send_sem.at[i],
            recv_sem=recv_sem.at[i],
            device_id={"gx": gx + dx, "gy": gy + dy},
            device_id_type=MESH,
        )

    for i, (dx, dy) in enumerate(SIDES):

        @pl.when(have(dx, dy, 0))
        def _():
            side_copy(i).start()

        @pl.when(jnp.logical_not(have(-dx, -dy, 0)))
        def _():
            shape = (4 if dx else 32, 8 if dy else 128, 128)
            ext[dst_x[dx], dst_y[dy], :] = jnp.zeros(shape, F32)

    mine.wait()
    for i, (dx, dy) in enumerate(SIDES):

        @pl.when(have(-dx, -dy, 0))
        def _():
            side_copy(i).wait_recv()

    lane = iota((40, 128), 1)
    slot = lane % 8
    low = slot < 4
    j_of = 15 - lane // 8

    flat = ext.reshape(40 * 144, 128)

    def pack_planes(n, _):
        lane8 = iota((8, 128), 1) // 8
        for i in range(8):
            x = n * 8 + i
            acc = jnp.zeros((8, 128), F32)
            for j in range(16):
                rows = pltpu.roll(ext[x, pl.ds(4 + j, 8, stride=16), :], (124 - 8 * j) % 128, axis=1)
                acc = jnp.where(lane8 == 15 - j, rows, acc)
            own[pl.ds(x, 8, stride=40), :] = acc
        acc = jnp.zeros((8, 128), F32)
        for j in range(8):
            rows = pltpu.roll(flat[pl.ds(n * 8 * 144 + 132 + j, 8, stride=144), :], (124 - 8 * j) % 128, axis=1)
            acc = jnp.where(lane8 == 15 - j, rows, acc)
        own[pl.ds(320 + n * 8, 8), :] = acc
        return 0

    lax.fori_loop(0, 5, pack_planes, 0)

    def mine_at(g):
        return own[40 * g : 40 * g + 40, :]

    for m in range(5):
        this, that = mine_at(m if m < 4 else 8), mine_at(m + 4)
        pk_out[0, m] = jnp.where(low, this, pltpu.roll(that, 4, axis=1))
        pk_out[1, m] = jnp.where(low, pltpu.roll(this, 124, axis=1), that)

    def z_copy(i):
        return pltpu.make_async_remote_copy(
            src_ref=pk_out.at[i],
            dst_ref=pk_in.at[i],
            send_sem=zsend.at[i],
            recv_sem=zrecv.at[i],
            device_id={"gz": gz + (1 - 2 * i)},
            device_id_type=MESH,
        )

    for i in range(2):
        d = 1 - 2 * i

        @pl.when(have(0, 0, d))
        def _():
            z_copy(i).start()

        @pl.when(jnp.logical_not(have(0, 0, -d)))
        def _():
            pk_in[i] = jnp.zeros((5, 40, 128), F32)

    def make_band(k, _):
        c = off[k, 2]
        row, col = iota((128, 256), 0), iota((128, 256), 1)
        fwd = col < 128
        spot = jnp.where(fwd, col, col - 128 - c)
        hit = jnp.where(jnp.abs(row - spot) <= 1, -1.0, 0.0)
        s = row % 8
        edge_z = jnp.where(s < 4, s - 4, s + 124)
        edge = jnp.where(jnp.abs(edge_z - spot) <= 1, -1.0, 0.0)
        first = jnp.where(c > 0, 5, 0)
        at = gz * SZ + jnp.where(fwd, col + c, spot)
        beyond = jnp.logical_or(at < 0, at >= nz * SZ)
        edge = jnp.where(s == first, jnp.where(fwd, -BIG, 0.0), edge)
        edge = jnp.where(s == first + 1, jnp.where(fwd, 0.0, -BIG), edge)
        edge = jnp.where(s == first + 2, jnp.where(beyond, -BIG, 0.0), edge)
        hit, edge = hit.astype(BF16), edge.astype(BF16)
        band[k, 0:128, :] = hit
        band[k, 128:256, :] = hit
        band[k, 256:384, :] = edge
        band[k, 384:512, :] = edge
        return 0

    lax.fori_loop(0, PAIRS, make_band, 0)
    for i in range(BLOCK):
        for xs in (xa, xb):
            xs[i, 0:8, :] = jnp.zeros((8, 128), F32)
            xs[i, 144:168, :] = jnp.zeros((24, 128), F32)
    re[...] = jnp.zeros_like(re)
    sv[40] = jnp.zeros((144, 128), F32)
    hal[40] = jnp.zeros((152, 128), F32)
    fs[:, 0] = jnp.zeros((3, 40, 128), F32)
    fs[:, GROUPS + 1] = jnp.zeros((3, 40, 128), F32)
    de[...] = jnp.zeros_like(de)

    def scale(x, _):
        sv[x] = ext[x] * KAPPA
        return 0

    lax.fori_loop(0, 40, scale, 0)

    row, col = iota((128, 128), 0), iota((128, 128), 1)
    spread_one = jnp.where((row % 8 + 124) % 128 == col, 1.0, 0.0)
    spread_one = spread_one.astype(BF16)
    spread = jnp.concatenate([spread_one, spread_one], axis=0)

    for i in range(2):
        d = 1 - 2 * i

        @pl.when(have(0, 0, -d))
        def _():
            z_copy(i).wait_recv()

    for m in range(5):
        left, right = pk_in[0, m], pk_in[1, m]
        parts = [(m if m < 4 else 8, left, pltpu.roll(right, 4, axis=1))]
        if m < 4:
            parts.append((m + 4, pltpu.roll(left, 124, axis=1), right))
        for g, from_left, from_right in parts:
            mid = mine_at(g)
            qh[g] = jnp.where(low, from_left, from_right) * KAPPA
            ql[g] = jnp.where(low, from_left, mid) * KAPPA
            qr[g] = jnp.where(low, mid, from_right) * KAPPA

    diag = iota((16, 128), 1) // 8 == 15 - iota((16, 128), 0)
    none = jnp.zeros((), BF16)

    def halo_planes(n, _):
        for i in range(4):
            x = n * 4 + i
            left = []
            for g in range(GROUPS):
                field = jnp.broadcast_to(qh[g, pl.ds(x, 1), :], (16, 128))
                high = field.astype(BF16)
                rest = (field - high.astype(F32)).astype(BF16)
                left.append(jnp.concatenate([jnp.where(diag, high, none), jnp.where(diag, rest, none)], axis=1))
            left = jnp.concatenate(left, axis=0)
            hal[x, 4:148, :] = jnp.dot(left, spread, preferred_element_type=F32)
        return 0

    lax.fori_loop(0, 10, halo_planes, 0)

    def edges(k, _):
        a, b, c = off[k, 0], off[k, 1], off[k, 2]
        turn = lax.rem(128 + 8 * b - c, 128)
        step = jnp.where(b < 0, -1, 1)
        for g in range(GROUPS):
            re[g + 1, 0:40, :] = jnp.where(low, pltpu.roll(ql[g], turn, axis=1), pltpu.roll(qr[g], turn, axis=1))
        inner = jnp.logical_and(j_of + b >= 0, j_of + b < 16)
        for g in range(GROUPS):
            partner = jnp.where(inner, re[g + 1, pl.ds(a, 40), :], re[g + 1 + step, pl.ds(a, 40), :])
            diff = qh[g] - partner
            de[g, 0:40, :] = diff * diff
        for g in range(GROUPS):
            field = de[g, 0:40, :] + de[g, 1:41, :] + de[g, 2:42, :]
            fs[0, g + 1] = field
            fs[1, g + 1] = pltpu.roll(field, 8, axis=1)
            fs[2, g + 1] = pltpu.roll(field, 120, axis=1)

        first = jnp.where(c > 0, 5, 0)
        x_at = gx * SX + iota((40, 128), 0) - 3
        x_to = x_at + a
        is_to, is_at, is_one = slot == first, slot == first + 1, slot == first + 2
        off_x_to = jnp.logical_or(x_to < 0, x_to >= nx * SX)
        off_x_at = jnp.logical_or(x_at < 0, x_at >= nx * SX)
        is_flag = jnp.logical_or(jnp.logical_or(is_to, is_at), is_one)
        flag_x = jnp.logical_or(
            jnp.logical_or(jnp.logical_and(is_to, off_x_to), jnp.logical_and(is_at, off_x_at)), is_one
        )
        y_lane = gy * SY - 4 + j_of + jnp.where(is_to, b, 0)
        flag_x = jnp.where(flag_x, 1.0, 0.0)
        for g in range(GROUPS):
            up = jnp.where(lane >= 8, fs[1, g + 1], fs[1, g + 2])
            down = jnp.where(lane < 120, fs[2, g + 1], fs[2, g])
            field = fs[0, g + 1] + up + down
            y = y_lane + 16 * g
            flag = jnp.where(jnp.logical_or(y < 0, y >= ny * SY), 1.0, flag_x)
            field = jnp.where(is_flag, flag, field)
            high = field.astype(BF16).astype(F32)
            eh[k, g] = high
            el[k, g] = field - high
        return 0

    lax.fori_loop(0, PAIRS, edges, 0)

    lane8 = iota((8, 128), 1)

    def shifts(k):
        a, b, c = off[k, 0], off[k, 1], off[k, 2]
        turn = lax.rem(128 - c, 128)
        beyond = jnp.logical_or(lane8 < c, lane8 >= 128 + c)

        def square(x, t):
            rows = pl.ds(b + (8 * t + 4), 8)
            partner = pltpu.roll(jnp.where(beyond, hal[x + a, rows, :], sv[x + a, rows, :]), turn, axis=1)
            near[k, x, 8 * t : 8 * t + 8, :] = partner
            diff = sv[x, 8 * t + 4 : 8 * t + 12, :] - partner
            return diff * diff

        return square

    def begin(k, _):
        square = shifts(k)
        for t in range(17):
            d0, d1 = square(0, t), square(1, t)
            carry[k, 0, 8 * t : 8 * t + 8, :] = d0 + d1
            carry[k, 1, 8 * t : 8 * t + 8, :] = d1
        return 0

    lax.fori_loop(0, PAIRS, begin, 0)

    def field_step(s, xs):
        k = s // STEPS
        p = (s % STEPS) * BLOCK
        square = shifts(k)
        for t in range(17):
            rows = slice(8 * t, 8 * t + 8)
            d = [square(p + 2 + i, t) for i in range(BLOCK)]
            d01, d23, d45 = d[0] + d[1], d[2] + d[3], d[4] + d[5]
            sums = (carry[k, 0, rows, :] + d[0], carry[k, 1, rows, :] + d01, d01 + d[2], d[1] + d23, d23 + d[4], d[3] + d45)
            for i in range(BLOCK):
                xs[i, 8 + 8 * t : 16 + 8 * t, :] = sums[i]
            carry[k, 0, rows, :] = d45
            carry[k, 1, rows, :] = d[5]

    def weight_step(s, xs):
        k = s // STEPS
        p = (s % STEPS) * BLOCK
        for i in range(0, BLOCK, TOGETHER):
            left = []
            for h in range(i, i + TOGETHER):
                for g in range(GROUPS):
                    r = 8 + 16 * g
                    field = xs[h, r - 1 : r + 15, :] + xs[h, r : r + 16, :] + xs[h, r + 1 : r + 17, :]
                    high = field.astype(BF16)
                    rest = (field - high.astype(F32)).astype(BF16)
                    e_high = jnp.broadcast_to(eh[k, g, pl.ds(p + h, 1), :], (16, 128)).astype(BF16)
                    e_rest = jnp.broadcast_to(el[k, g, pl.ds(p + h, 1), :], (16, 128)).astype(BF16)
                    left.append(
                        jnp.concatenate(
                            [high, rest, jnp.where(diag, e_high, none), jnp.where(diag, e_rest, none)], axis=1
                        )
                    )
            left = jnp.concatenate(left, axis=0)
            weight = jnp.exp2(jnp.dot(left, band[k], preferred_element_type=F32))
            for h in range(TOGETHER):
                w1[k, p + i + h] = weight[144 * h : 144 * h + 136, 0:128]
                w2[k, p + i + h] = weight[144 * h : 144 * h + 136, 128:256]

    field_step(0, xa)

    def two_steps(n, _):
        s = 2 * n
        field_step(s + 1, xb)
        weight_step(s, xa)
        field_step(jnp.minimum(s + 2, PAIRS * STEPS - 1), xa)
        weight_step(s + 1, xb)
        return 0

    lax.fori_loop(0, PAIRS * STEPS // 2, two_steps, 0)

    def finish(x, _):
        for t in range(16):
            y = 8 * t
            num = sv[x + 4, y + 8 : y + 16, :]
            den = jnp.ones((8, 128), F32)
            for k in range(PAIRS):
                c = off[k, 2]
                from_x = x - off[k, 0]
                up = jnp.maximum(8 - off[k, 1], 5)
                up_w = jnp.maximum(4 - off[k, 1], 1)
                beyond = jnp.logical_or(lane8 < 0 - c, lane8 >= 128 - c)
                rows = pl.ds(up + y, 8)
                back = jnp.where(beyond, hal[from_x + 4, rows, :], sv[from_x + 4, rows, :])
                back = pltpu.roll(back, lax.rem(128 + c, 128), axis=1)
                fore_w = w1[k, x + 3, y + 4 : y + 12, :]
                back_w = w2[k, from_x + 3, pl.ds(up_w + y, 8), :]
                num = num + fore_w * near[k, x + 4, y + 4 : y + 12, :] + back_w * back
                den = den + fore_w + back_w
            out[x, y : y + 8, :] = num / (den * KAPPA)
        return 0

    lax.fori_loop(0, SX, finish, 0)

    for i, (dx, dy) in enumerate(SIDES):

        @pl.when(have(dx, dy, 0))
        def _():
            side_copy(i).wait_send()

    for i in range(2):

        @pl.when(have(0, 0, 1 - 2 * i))
        def _():
            z_copy(i).wait_send()


def local(counts, volume, offsets):
    return pl.pallas_call(
        functools.partial(kernel, counts),
        out_shape=jax.ShapeDtypeStruct((SX, SY, SZ), F32),
        in_specs=[pl.BlockSpec(memory_space=pltpu.SMEM), pl.BlockSpec(memory_space=pl.ANY)],
        out_specs=pl.BlockSpec(memory_space=pltpu.VMEM),
        scratch_shapes=[
            pltpu.VMEM((40, 144, 128), F32),
            pltpu.VMEM((41, 144, 128), F32),
            pltpu.VMEM((41, 152, 128), F32),
            pltpu.VMEM((PAIRS, 38, 136, 128), F32),
            pltpu.VMEM((GROUPS * 40, 128), F32),
            pltpu.VMEM((2, 5, 40, 128), F32),
            pltpu.VMEM((2, 5, 40, 128), F32),
            pltpu.VMEM((GROUPS, 40, 128), F32),
            pltpu.VMEM((GROUPS, 40, 128), F32),
            pltpu.VMEM((GROUPS, 40, 128), F32),
            pltpu.VMEM((GROUPS + 2, 48, 128), F32),
            pltpu.VMEM((GROUPS, 48, 128), F32),
            pltpu.VMEM((3, GROUPS + 2, 40, 128), F32),
            pltpu.VMEM((PAIRS, GROUPS, 40, 128), F32),
            pltpu.VMEM((PAIRS, GROUPS, 40, 128), F32),
            pltpu.VMEM((PAIRS, 512, 256), BF16),
            pltpu.VMEM((BLOCK, 168, 128), F32),
            pltpu.VMEM((BLOCK, 168, 128), F32),
            pltpu.VMEM((PAIRS, 2, 136, 128), F32),
            pltpu.VMEM((PAIRS, 36, 136, 128), F32),
            pltpu.VMEM((PAIRS, 36, 136, 128), F32),
            pltpu.SemaphoreType.DMA((8,)),
            pltpu.SemaphoreType.DMA((8,)),
            pltpu.SemaphoreType.DMA((2,)),
            pltpu.SemaphoreType.DMA((2,)),
            pltpu.SemaphoreType.DMA,
        ],
        compiler_params=pltpu.CompilerParams(
            collective_id=0, has_side_effects=True, vmem_limit_bytes=62 * 1024 * 1024
        ),
    )(offsets, volume)


def solution(mesh):
    counts = (mesh.shape["gx"], mesh.shape["gy"], mesh.shape["gz"])
    spec = P("gx", "gy", "gz")
    return jax.shard_map(
        functools.partial(local, counts), mesh=mesh, in_specs=(spec, P()), out_specs=spec, check_vma=False
    )
```

time: 86.9 us -> 44.7 us (0.51)
  Pallas kernels: 83.6 us -> 41.4 us
    pallas_call x1, Pallas kernels: 83.6 us -> 41.4 us  [local(): pl.pallas_call(functools.partial(kernel, counts), out_shape=jax.ShapeDtyp...]
where the time goes in v1:
time: 44.7 us; the launch traced here: 44.5 us
  Pallas kernels  41.4 us (93%)
  local copies, waits for them, and re-layouts  3.14 us (7%)
    pallas_call x1, Pallas kernels, local(): pl.pallas_call(functools.partial(kernel, counts), out_shape=jax.ShapeDtyp...  41.4 us
    unnamed x1, local copies, waits for them, and re-layouts  3.14 us

profile of v1, /device:TPU:1, one launch (start us, length us, event | category | flops | bytes accessed | tf_op | source)
XLA Modules:
  0.0 44.5 jit_solution(13208391958531381355)
XLA Ops:
  0.0 41.4 %shard_map.28 = f32[32,128,128]{2,1,0:T(8,128)} custom-call(s32[4,3]{1,0:T(4,128)} %off.1, f32[32,128,128]{2,1,0:T(8,128)} %v.1), custom_call_target="tpu_custom_call" | custom-call | tf_op jit(solution)/shard_map/pallas_call | solution.py:384
  41.4 3.1 %copy.4 = f32[32,128,128]{2,1,0:T(8,128)} copy(f32[32,128,128]{2,1,0:T(8,128)} %shard_map.28) | data formatting | bytes 4194304

commit v2 on v1

v2 whole, which is shorter than its diff:
```python
import functools
import math

import jax
import jax.numpy as jnp
from jax import lax
from jax.experimental import pallas as pl
from jax.experimental.pallas import tpu as pltpu
from jax.sharding import PartitionSpec as P

SX, SY, SZ = 32, 128, 128
PAIRS = 4
KAPPA = math.sqrt(math.log2(math.e) / 54.0)
BIG = 16384.0
GROUPS = 9
BLOCK = 6
TOGETHER = 3
F32 = jnp.float32
BF16 = jnp.bfloat16
MESH = pl.DeviceIdType.MESH

SIDES = [(dx, dy) for dx in (-1, 0, 1) for dy in (-1, 0, 1) if (dx, dy) != (0, 0)]


FRIENDS = [(dx, dy, 0) for dx, dy in SIDES] + [(0, dy, dz) for dy in (-1, 0, 1) for dz in (-1, 1)]


def iota(shape, dim):
    return lax.broadcasted_iota(jnp.int32, shape, dim)


def kernel(counts, off, v, out, ext, sv, hal, near, own, pk_out, pk_in, yz_out, yz_in, xe_out, xe_in, qh, qm, re, de, fs,
           eh, el, band, xa, xb, carry, w1, w2, t2, done, send_sem, recv_sem, own_sem, out_sem):
    nx, ny, nz = counts
    gx, gy, gz = lax.axis_index("gx"), lax.axis_index("gy"), lax.axis_index("gz")

    def have(dx, dy, dz):
        ok = True
        for at, d, n in ((gx, dx, nx), (gy, dy, ny), (gz, dz, nz)):
            if d > 0:
                ok = jnp.logical_and(ok, at + d < n)
            elif d < 0:
                ok = jnp.logical_and(ok, at + d >= 0)
        return ok

    mine = pltpu.make_async_copy(v, ext.at[4:36, 8:136, :], own_sem)
    mine.start()

    barrier = pltpu.get_barrier_semaphore()
    total = jnp.int32(0)
    for dx, dy, dz in FRIENDS:
        ok = have(dx, dy, dz)
        total = total + ok.astype(jnp.int32)

        @pl.when(ok)
        def _():
            pl.semaphore_signal(barrier, inc=1, device_id={"gx": gx + dx, "gy": gy + dy, "gz": gz + dz}, device_id_type=MESH)

    src_x = {1: pl.ds(28, 4), -1: pl.ds(0, 4), 0: pl.ds(0, 32)}
    dst_x = {1: pl.ds(0, 4), -1: pl.ds(36, 4), 0: pl.ds(4, 32)}
    src_y = {1: pl.ds(120, 8), -1: pl.ds(0, 8), 0: pl.ds(0, 128)}
    dst_y = {1: pl.ds(0, 8), -1: pl.ds(136, 8), 0: pl.ds(8, 128)}

    def copy(way, src, dst, n):
        return pltpu.make_async_remote_copy(
            src_ref=src,
            dst_ref=dst,
            send_sem=send_sem.at[n],
            recv_sem=recv_sem.at[n],
            device_id={"gx": gx + way[0], "gy": gy + way[1], "gz": gz + way[2]},
            device_id_type=MESH,
        )

    side = {}
    for i, (dx, dy) in enumerate(SIDES):
        place = ext.at[dst_x[dx], dst_y[dy], :]
        side[dx, dy] = ((dx, dy, 0), v.at[src_x[dx], src_y[dy], :], place, i)
    across = [((0, 0, 1 - 2 * i), pk_out.at[i], pk_in.at[i], 8 + i) for i in range(2)]
    corner = [
        ((0, 1 - 2 * j, 1 - 2 * i), yz_out.at[j], yz_in.at[i, j], 10 + 2 * i + j) for i in range(2) for j in range(2)
    ]
    ends = [((1 - 2 * i, 0, 0), xe_out.at[i], xe_in.at[i], 14 + i) for i in range(2)]
    slabs = [side[key] for key in side if key[0] != 0]
    strips = [side[key] for key in side if key[0] == 0]

    def start(item):
        @pl.when(have(*item[0]))
        def _():
            copy(*item).start()

    def clear(item):
        way, place = item[0], item[2]

        @pl.when(jnp.logical_not(have(-way[0], -way[1], -way[2])))
        def _():
            place[...] = jnp.zeros(place.shape, F32)

    def arrive(item):
        way = item[0]

        @pl.when(have(-way[0], -way[1], -way[2]))
        def _():
            copy(*item).wait_recv()

    def leave(item):
        @pl.when(have(*item[0]))
        def _():
            copy(*item).wait_send()

    mine.wait()

    lane = iota((40, 128), 1)
    slot = lane % 8
    low = slot < 4
    j_of = 15 - lane // 8
    lane32 = iota((32, 128), 1)
    low32 = lane32 % 8 < 4
    lane8 = iota((8, 128), 1)
    low8 = lane8 % 8 < 4

    def pack_planes(n, _):
        for i in range(8):
            x = n * 8 + i
            acc = jnp.zeros((8, 128), F32)
            for j in range(16):
                first = 4 + j if j >= 4 else 20 + j
                rows = pltpu.roll(ext[x + 4, pl.ds(first, 8, stride=16), :], (124 - 8 * j) % 128, axis=1)
                acc = jnp.where(lane8 // 8 == 15 - j, rows, acc)
            own[pl.ds(x, 8, stride=32), :] = acc
        return 0

    lax.fori_loop(0, 4, pack_planes, 0)

    def mine_at(i):
        return own[32 * i : 32 * i + 32, :]

    for m in range(4):
        this, that = mine_at(m), mine_at(m + 4)
        pk_out[0, m] = jnp.where(low32, this, pltpu.roll(that, 4, axis=1))
        pk_out[1, m] = jnp.where(low32, pltpu.roll(this, 124, axis=1), that)
    for j, (block, lanes) in enumerate(((7, 96), (0, 64))):
        acc = jnp.zeros((8, 128), F32)
        for q in range(4):
            rows = own[32 * block + 8 * q : 32 * block + 8 * q + 8, :]
            acc = jnp.where(lane8 // 32 == q, pltpu.roll(rows, (32 * q - lanes) % 128, axis=1), acc)
        yz_out[j] = acc
    pl.semaphore_wait(barrier, total)
    for item in corner + across + strips + slabs:
        start(item)

    for item in strips + across + corner + slabs + ends:
        clear(item)

    def make_band(k, _):
        c = off[k, 2]
        row, col = iota((128, 256), 0), iota((128, 256), 1)
        fwd = col < 128
        spot = jnp.where(fwd, col, col - 128 - c)
        hit = jnp.where(jnp.abs(row - spot) <= 1, -1.0, 0.0)
        s = row % 8
        edge_z = jnp.where(s < 4, s - 4, s + 124)
        edge = jnp.where(jnp.abs(edge_z - spot) <= 1, -1.0, 0.0)
        first = jnp.where(c > 0, 5, 0)
        at = gz * SZ + jnp.where(fwd, col + c, spot)
        beyond = jnp.logical_or(at < 0, at >= nz * SZ)
        edge = jnp.where(s == first, jnp.where(fwd, -BIG, 0.0), edge)
        edge = jnp.where(s == first + 1, jnp.where(fwd, 0.0, -BIG), edge)
        edge = jnp.where(s == first + 2, jnp.where(beyond, -BIG, 0.0), edge)
        hit, edge = hit.astype(BF16), edge.astype(BF16)
        band[k, 0:128, :] = hit
        band[k, 128:256, :] = hit
        band[k, 256:384, :] = edge
        band[k, 384:512, :] = edge
        return 0

    lax.fori_loop(0, PAIRS, make_band, 0)
    for i in range(BLOCK):
        for xs in (xa, xb):
            xs[i, 0:8, :] = jnp.zeros((8, 128), F32)
            xs[i, 144:168, :] = jnp.zeros((24, 128), F32)
    re[...] = jnp.zeros_like(re)
    de[...] = jnp.zeros_like(de)
    for x in (0, 1, 2, 3, 36, 37, 38, 39, 40):
        sv[x] = jnp.zeros((144, 128), F32)
        hal[x] = jnp.zeros((152, 128), F32)
    for g in range(GROUPS):
        qh[g] = jnp.zeros((40, 128), F32)
        qm[g] = jnp.zeros((40, 128), F32)
    fs[:, 0] = jnp.zeros((3, 40, 128), F32)
    fs[:, GROUPS + 1] = jnp.zeros((3, 40, 128), F32)
    carry[...] = jnp.zeros_like(carry)

    row, col = iota((128, 128), 0), iota((128, 128), 1)
    spread_one = jnp.where((row % 8 + 124) % 128 == col, 1.0, 0.0).astype(BF16)
    spread = jnp.concatenate([spread_one, spread_one], axis=0)

    def scale(n, _):
        for i in range(4):
            x = 4 + 4 * n + i
            sv[x, 8:136, :] = ext[x, 8:136, :] * KAPPA
        return 0

    lax.fori_loop(0, 8, scale, 0)
    for item in strips:
        arrive(item)
    for x in range(4, 36):
        sv[x, 0:8, :] = ext[x, 0:8, :] * KAPPA
        sv[x, 136:144, :] = ext[x, 136:144, :] * KAPPA

    flat = ext.reshape(40 * 144, 128)
    beyond_low, beyond_high = [], []
    for q in range(4):
        acc_low, acc_high = jnp.zeros((8, 128), F32), jnp.zeros((8, 128), F32)
        base = (4 + 8 * q) * 144
        for j in range(4):
            rows = pltpu.roll(flat[pl.ds(base + 4 + j, 8, stride=144), :], (124 - 8 * j) % 128, axis=1)
            acc_low = jnp.where(lane8 // 8 == 15 - j, rows, acc_low)
            rows = pltpu.roll(flat[pl.ds(base + 136 + j, 8, stride=144), :], (92 - 8 * j) % 128, axis=1)
            acc_high = jnp.where(lane8 // 8 == 11 - j, rows, acc_high)
        beyond_low.append(acc_low)
        beyond_high.append(acc_high)
    mids = [jnp.concatenate(beyond_low, axis=0)] + [mine_at(i) for i in range(8)] + [jnp.concatenate(beyond_high, axis=0)]
    for g in range(GROUPS):
        qm[g, 4:36, :] = jnp.where(lane32 < 96, mids[g + 1], mids[g]) * KAPPA

    for item in across + corner:
        arrive(item)
    halos = [None] * 10
    for j, (block, lanes) in enumerate(((0, 96), (9, 64))):
        both = jnp.where(low8, yz_in[0, j], yz_in[1, j])
        parts = [pltpu.roll(both, (lanes - 32 * q) % 128, axis=1) for q in range(4)]
        halos[block] = jnp.concatenate(parts, axis=0)
    for m in range(4):
        left, right = pk_in[0, m], pk_in[1, m]
        halos[1 + m] = jnp.where(low32, left, pltpu.roll(right, 4, axis=1))
        halos[5 + m] = jnp.where(low32, pltpu.roll(left, 124, axis=1), right)
    for g in range(GROUPS):
        qh[g, 4:36, :] = jnp.where(lane32 < 96, halos[g + 1], halos[g]) * KAPPA
    for g in range(GROUPS):
        for i, first in enumerate((32, 4)):
            xe_out[i, g, 0:4, :] = qh[g, first : first + 4, :]
            xe_out[i, g, 4:8, :] = qm[g, first : first + 4, :]
    for item in ends:
        start(item)

    diag = iota((16, 128), 1) // 8 == 15 - iota((16, 128), 0)
    none = jnp.zeros((), BF16)

    def halo_planes(planes):
        left = []
        for x in planes:
            for g in range(GROUPS):
                field = jnp.broadcast_to(qh[g, pl.ds(x, 1), :], (16, 128))
                high = field.astype(BF16)
                rest = (field - high.astype(F32)).astype(BF16)
                left.append(jnp.concatenate([jnp.where(diag, high, none), jnp.where(diag, rest, none)], axis=1))
        left = jnp.concatenate(left, axis=0)
        spot = jnp.dot(left, spread, preferred_element_type=F32)
        for i, x in enumerate(planes):
            hal[x, 4:148, :] = spot[144 * i : 144 * i + 144]

    def edges(spans_d, spans_p, planes):
        def one(k, _):
            edge_pair(k, spans_d, spans_p)
            halo_planes(planes(k))
            return 0

        lax.fori_loop(0, PAIRS, one, 0)

    def edge_pair(k, spans_d, spans_p):
        a, b, c = off[k, 0], off[k, 1], off[k, 2]
        turn = lax.rem(128 + 8 * b - c, 128)
        step = jnp.where(b < 0, -1, 1)
        same = low == (slot - c < 4)
        for g in range(GROUPS):
            re[g + 1, 0:40, :] = pltpu.roll(jnp.where(same, qh[g], qm[g]), turn, axis=1)

        def lanes_of(n):
            lane_n = iota((n, 128), 1)
            return lane_n, lane_n % 8, 15 - lane_n // 8

        for first, n in spans_d:
            _, _, j_n = lanes_of(n)
            inner = jnp.logical_and(j_n + b >= 0, j_n + b < 16)
            for g in range(GROUPS):
                rows = pl.ds(a + first, n)
                diff = qh[g, first : first + n, :] - jnp.where(inner, re[g + 1, rows, :], re[g + 1 + step, rows, :])
                de[g, first : first + n, :] = diff * diff
        flag0 = jnp.where(c > 0, 5, 0)
        for first, n in spans_p:
            lane_n, slot_n, j_n = lanes_of(n)
            for g in range(GROUPS):
                field = de[g, first : first + n, :] + de[g, first + 1 : first + n + 1, :] + de[g, first + 2 : first + n + 2, :]
                fs[0, g + 1, first : first + n, :] = field
                fs[1, g + 1, first : first + n, :] = pltpu.roll(field, 8, axis=1)
                fs[2, g + 1, first : first + n, :] = pltpu.roll(field, 120, axis=1)
            x_at = gx * SX + iota((n, 128), 0) + (first - 3)
            is_to, is_at, is_one = slot_n == flag0, slot_n == flag0 + 1, slot_n == flag0 + 2
            x = x_at + jnp.where(is_to, a, 0)
            off_x = jnp.logical_or(is_one, jnp.logical_or(x < 0, x >= nx * SX))
            flag_x = jnp.where(off_x, 1.0, 0.0)
            is_flag = jnp.logical_and(slot_n >= flag0, slot_n < flag0 + 3)
            y_lane = gy * SY - 4 + j_n + jnp.where(is_to, b, 0)
            for g in range(GROUPS):
                rows = slice(first, first + n)
                up = jnp.where(lane_n >= 8, fs[1, g + 1, rows, :], fs[1, g + 2, rows, :])
                down = jnp.where(lane_n < 120, fs[2, g + 1, rows, :], fs[2, g, rows, :])
                field = fs[0, g + 1, rows, :] + up + down
                flag = flag_x
                if g in (0, GROUPS - 1):
                    y = y_lane + 16 * g
                    flag = jnp.where(jnp.logical_or(y < 0, y >= ny * SY), 1.0, flag_x)
                field = jnp.where(is_flag, flag, field)
                high = field.astype(BF16).astype(F32)
                eh[k, g, rows, :] = high
                el[k, g, rows, :] = field - high

    edges([(0, 32)], [(0, 32)], lambda k: [4 + 8 * k + i for i in range(8)])


    def shifts(k):
        a, b, c = off[k, 0], off[k, 1], off[k, 2]
        turn = lax.rem(128 - c, 128)
        beyond = jnp.logical_or(lane8 < c, lane8 >= 128 + c)

        def square(x, t):
            rows = pl.ds(b + (8 * t + 4), 8)
            partner = pltpu.roll(jnp.where(beyond, hal[x + a, rows, :], sv[x + a, rows, :]), turn, axis=1)
            near[k, x, 8 * t : 8 * t + 8, :] = partner
            diff = sv[x, 8 * t + 4 : 8 * t + 12, :] - partner
            return diff * diff

        return square

    def begin(p, slot):
        def one(k, _):
            square = shifts(k)
            for t in range(17):
                d0, d1 = square(p, t), square(p + 1, t)
                carry[slot, k, 0, 8 * t : 8 * t + 8, :] = d0 + d1
                carry[slot, k, 1, 8 * t : 8 * t + 8, :] = d1
            return 0

        lax.fori_loop(0, PAIRS, one, 0)

    def field_step(k, n, slot, xs):
        p = n * BLOCK
        square = shifts(k)
        for t in range(17):
            rows = slice(8 * t, 8 * t + 8)
            d = [square(p + 2 + i, t) for i in range(BLOCK)]
            d01, d23, d45 = d[0] + d[1], d[2] + d[3], d[4] + d[5]
            sums = (carry[slot, k, 0, rows, :] + d[0], carry[slot, k, 1, rows, :] + d01, d01 + d[2], d[1] + d23, d23 + d[4], d[3] + d45)
            for i in range(BLOCK):
                xs[i, 8 + 8 * t : 16 + 8 * t, :] = sums[i]
            carry[slot, k, 0, rows, :] = d45
            carry[slot, k, 1, rows, :] = d[5]

    def weight_step(k, n, xs):
        p = n * BLOCK
        c = off[k, 2]
        beyond = jnp.logical_or(lane8 < 0 - c, lane8 >= 128 - c)
        turn = lax.rem(128 + c, 128)
        for i in range(0, BLOCK, TOGETHER):
            left = []
            for h in range(i, i + TOGETHER):
                for g in range(GROUPS):
                    r = 8 + 16 * g
                    field = xs[h, r - 1 : r + 15, :] + xs[h, r : r + 16, :] + xs[h, r + 1 : r + 17, :]
                    high = field.astype(BF16)
                    rest = (field - high.astype(F32)).astype(BF16)
                    e_high = jnp.broadcast_to(eh[k, g, pl.ds(p + h, 1), :], (16, 128)).astype(BF16)
                    e_rest = jnp.broadcast_to(el[k, g, pl.ds(p + h, 1), :], (16, 128)).astype(BF16)
                    left.append(
                        jnp.concatenate(
                            [high, rest, jnp.where(diag, e_high, none), jnp.where(diag, e_rest, none)], axis=1
                        )
                    )
            left = jnp.concatenate(left, axis=0)
            weight = jnp.exp2(jnp.dot(left, band[k], preferred_element_type=F32))
            for h in range(TOGETHER):
                w1[k, p + i + h] = weight[144 * h : 144 * h + 136, 0:128]
                w2[k, p + i + h] = weight[144 * h : 144 * h + 136, 128:256]
                for t in range(17):
                    rows, at = slice(8 * t, 8 * t + 8), slice(8 * t + 4, 8 * t + 12)
                    x = p + i + h + 1
                    back = pltpu.roll(jnp.where(beyond, hal[x, at, :], sv[x, at, :]), turn, axis=1)
                    t2[k, p + i + h, rows, :] = back * weight[144 * h + 8 * t : 144 * h + 8 * t + 8, 128:256]

    def run(steps, place):
        def field(s, xs):
            k, n, slot = place(jnp.minimum(s, steps - 1))
            field_step(k, n, jnp.where(s < steps, slot, 2), xs)

        def weigh(s, xs):
            k, n, _ = place(s)
            weight_step(k, n, xs)

        field(jnp.int32(0), xa)

        def two_steps(i, _):
            s = 2 * i
            field(s + 1, xb)
            weigh(s, xa)
            field(s + 2, xa)
            weigh(s + 1, xb)
            return 0

        lax.fori_loop(0, steps // 2, two_steps, 0)

    begin(BLOCK, 0)
    run(PAIRS * 4, lambda s: (s // 4, 1 + s % 4, 0))

    for item in slabs + ends:
        arrive(item)
    for x in (0, 1, 2, 3, 36, 37, 38, 39):
        sv[x] = ext[x] * KAPPA
    for g in range(GROUPS):
        for i, first in enumerate((0, 36)):
            qh[g, first : first + 4, :] = xe_in[i, g, 0:4, :]
            qm[g, first : first + 4, :] = xe_in[i, g, 4:8, :]

    edges([(0, 16), (24, 16)], [(0, 8), (24, 16)], lambda k: [k, k + 36])
    begin(0, 1)
    run(PAIRS * 2, lambda s: (s // 2, 5 * (s % 2), 1 - s % 2))

    w2f, t2f = w2.reshape(PAIRS * 36 * 136, 128), t2.reshape(PAIRS * 36 * 136, 128)
    froms = [
        jnp.maximum((k * 36 + 3 - off[k, 0]) * 136 + 4 - off[k, 1], 1) for k in range(PAIRS)
    ]

    def finish(n, _):
        for x in (2 * n, 2 * n + 1):
            bases = [froms[k] + x * 136 for k in range(PAIRS)]
            for t in range(16):
                y = 8 * t
                num = sv[x + 4, y + 8 : y + 16, :]
                den = jnp.ones((8, 128), F32)
                for k in range(PAIRS):
                    rows = pl.ds(bases[k] + y, 8)
                    fore_w = w1[k, x + 3, y + 4 : y + 12, :]
                    num = num + (fore_w * near[k, x + 4, y + 4 : y + 12, :] + t2f[rows, :])
                    den = den + (fore_w + w2f[rows, :])
                done[x, y : y + 8, :] = num / (den * KAPPA)
            pltpu.make_async_copy(done.at[x], out.at[x], out_sem).start()
        return 0

    lax.fori_loop(0, SX // 2, finish, 0)
    pltpu.make_async_copy(done, out, out_sem).wait()
    for item in strips + across + corner + slabs + ends:
        leave(item)


PARTS = 4


def hand_over(src, dst, held, sems):
    n = SX // PARTS
    spans = [pl.ds(n * i, n) for i in range(PARTS)]
    ins = [pltpu.make_async_copy(src.at[span], held.at[span], sems.at[0, i]) for i, span in enumerate(spans)]
    outs = [pltpu.make_async_copy(held.at[span], dst.at[span], sems.at[1, i]) for i, span in enumerate(spans)]
    for item in ins:
        item.start()
    for first, then in zip(ins, outs):
        first.wait()
        then.start()
    for item in outs:
        item.wait()


def local(counts, volume, offsets):
    result = pl.pallas_call(
        functools.partial(kernel, counts),
        out_shape=jax.ShapeDtypeStruct((SX, SY, SZ), F32),
        in_specs=[pl.BlockSpec(memory_space=pltpu.SMEM), pl.BlockSpec(memory_space=pl.ANY)],
        out_specs=pl.BlockSpec(memory_space=pl.ANY),
        scratch_shapes=[
            pltpu.VMEM((40, 144, 128), F32),
            pltpu.VMEM((41, 144, 128), F32),
            pltpu.VMEM((41, 152, 128), F32),
            pltpu.VMEM((PAIRS, 38, 136, 128), F32),
            pltpu.VMEM((8 * 32, 128), F32),
            pltpu.VMEM((2, 4, 32, 128), F32),
            pltpu.VMEM((2, 4, 32, 128), F32),
            pltpu.VMEM((2, 8, 128), F32),
            pltpu.VMEM((2, 2, 8, 128), F32),
            pltpu.VMEM((2, GROUPS, 8, 128), F32),
            pltpu.VMEM((2, GROUPS, 8, 128), F32),
            pltpu.VMEM((GROUPS, 40, 128), F32),
            pltpu.VMEM((GROUPS, 40, 128), F32),
            pltpu.VMEM((GROUPS + 2, 48, 128), F32),
            pltpu.VMEM((GROUPS, 48, 128), F32),
            pltpu.VMEM((3, GROUPS + 2, 40, 128), F32),
            pltpu.VMEM((PAIRS, GROUPS, 40, 128), F32),
            pltpu.VMEM((PAIRS, GROUPS, 40, 128), F32),
            pltpu.VMEM((PAIRS, 512, 256), BF16),
            pltpu.VMEM((BLOCK, 168, 128), F32),
            pltpu.VMEM((BLOCK, 168, 128), F32),
            pltpu.VMEM((3, PAIRS, 2, 136, 128), F32),
            pltpu.VMEM((PAIRS, 36, 136, 128), F32),
            pltpu.VMEM((PAIRS, 36, 136, 128), F32),
            pltpu.VMEM((PAIRS, 36, 136, 128), F32),
            pltpu.VMEM((SX, SY, SZ), F32),
            pltpu.SemaphoreType.DMA((16,)),
            pltpu.SemaphoreType.DMA((16,)),
            pltpu.SemaphoreType.DMA,
            pltpu.SemaphoreType.DMA,
        ],
        compiler_params=pltpu.CompilerParams(
            collective_id=0, has_side_effects=True, vmem_limit_bytes=62 * 1024 * 1024
        ),
    )(offsets, volume)
    return pl.pallas_call(
        hand_over,
        out_shape=jax.ShapeDtypeStruct((SX, SY, SZ), F32),
        in_specs=[pl.BlockSpec(memory_space=pl.ANY)],
        out_specs=pl.BlockSpec(memory_space=pl.ANY),
        scratch_shapes=[pltpu.VMEM((SX, SY, SZ), F32), pltpu.SemaphoreType.DMA((2, PARTS))],
    )(result)


def solution(mesh):
    counts = (mesh.shape["gx"], mesh.shape["gy"], mesh.shape["gz"])
    spec = P("gx", "gy", "gz")
    return jax.shard_map(
        functools.partial(local, counts), mesh=mesh, in_specs=(spec, P()), out_specs=spec, check_vma=False
    )
```

time: 44.7 us -> 32.4 us (0.72)
  the two profiles are of different devices: /device:TPU:1 before, /device:TPU:44 now
where the time goes in v2:
time: 32.4 us; the launch traced here: 32.2 us
  Pallas kernels  32.2 us (99%)
    pallas_call x1, Pallas kernels, local(): pl.pallas_call(functools.partial(kernel, counts), out_shape=jax.ShapeDtyp...  29.8 us
    pallas_call x1, Pallas kernels, local(): pl.pallas_call(hand_over, out_shape=jax.ShapeDtypeStruct((SX, SY, SZ), F3...  2.42 us

profile of v2, /device:TPU:44, one launch (start us, length us, event | category | flops | bytes accessed | tf_op | source)
XLA Modules:
  0.0 32.2 jit_solution(12875138101088502867)
XLA Ops:
  0.0 29.8 %shard_map.28.src = f32[32,128,128]{2,1,0:T(8,128)} custom-call(s32[4,3]{1,0:T(4,128)} %off.1, f32[32,128,128]{2,1,0:T(8,128)} %v.1), custom_call_target="tpu_custom_call" | custom-call | tf_op jit(solution)/shard_map/pallas_call | solution.py:472
  29.8 2.4 %shard_map.29 = f32[32,128,128]{2,1,0:T(8,128)} custom-call(f32[32,128,128]{2,1,0:T(8,128)} %shard_map.28.src), custom_call_target="tpu_custom_call" | custom-call | tf_op jit(solution)/shard_map/pallas_call | solution.py:513

commit v3 on v2

--- a/solution.py
+++ b/solution.py
@@ -43,8 +43,12 @@
                 ok = jnp.logical_and(ok, at + d >= 0)
         return ok
 
-    mine = pltpu.make_async_copy(v, ext.at[4:36, 8:136, :], own_sem)
-    mine.start()
+    mine = [
+        pltpu.make_async_copy(v.at[pl.ds(8 * n, 8)], ext.at[pl.ds(4 + 8 * n, 8), pl.ds(8, 128), :], own_sem.at[n])
+        for n in range(4)
+    ]
+    for item in mine:
+        item.start()
 
     barrier = pltpu.get_barrier_semaphore()
     total = jnp.int32(0)
@@ -58,8 +62,8 @@
 
     src_x = {1: pl.ds(28, 4), -1: pl.ds(0, 4), 0: pl.ds(0, 32)}
     dst_x = {1: pl.ds(0, 4), -1: pl.ds(36, 4), 0: pl.ds(4, 32)}
-    src_y = {1: pl.ds(120, 8), -1: pl.ds(0, 8), 0: pl.ds(0, 128)}
-    dst_y = {1: pl.ds(0, 8), -1: pl.ds(136, 8), 0: pl.ds(8, 128)}
+    src_y = {1: pl.ds(124, 4), -1: pl.ds(0, 4), 0: pl.ds(0, 128)}
+    dst_y = {1: pl.ds(4, 4), -1: pl.ds(136, 4), 0: pl.ds(8, 128)}
 
     def copy(way, src, dst, n):
         return pltpu.make_async_remote_copy(
@@ -107,7 +111,6 @@
         def _():
             copy(*item).wait_send()
 
-    mine.wait()
 
     lane = iota((40, 128), 1)
     slot = lane % 8
@@ -118,7 +121,8 @@
     lane8 = iota((8, 128), 1)
     low8 = lane8 % 8 < 4
 
-    def pack_planes(n, _):
+    for n in range(4):
+        mine[n].wait()
         for i in range(8):
             x = n * 8 + i
             acc = jnp.zeros((8, 128), F32)
@@ -127,9 +131,6 @@
                 rows = pltpu.roll(ext[x + 4, pl.ds(first, 8, stride=16), :], (124 - 8 * j) % 128, axis=1)
                 acc = jnp.where(lane8 // 8 == 15 - j, rows, acc)
             own[pl.ds(x, 8, stride=32), :] = acc
-        return 0
-
-    lax.fori_loop(0, 4, pack_planes, 0)
 
     def mine_at(i):
         return own[32 * i : 32 * i + 32, :]
@@ -399,14 +400,18 @@
         field(jnp.int32(0), xa)
 
         def two_steps(i, _):
-            s = 2 * i
+            s = 4 * i
             field(s + 1, xb)
             weigh(s, xa)
             field(s + 2, xa)
             weigh(s + 1, xb)
+            field(s + 3, xb)
+            weigh(s + 2, xa)
+            field(s + 4, xa)
+            weigh(s + 3, xb)
             return 0
 
-        lax.fori_loop(0, steps // 2, two_steps, 0)
+        lax.fori_loop(0, steps // 4, two_steps, 0)
 
     begin(BLOCK, 0)
     run(PAIRS * 4, lambda s: (s // 4, 1 + s % 4, 0))
@@ -503,7 +508,7 @@
             pltpu.VMEM((SX, SY, SZ), F32),
             pltpu.SemaphoreType.DMA((16,)),
             pltpu.SemaphoreType.DMA((16,)),
-            pltpu.SemaphoreType.DMA,
+            pltpu.SemaphoreType.DMA((4,)),
             pltpu.SemaphoreType.DMA,
         ],
         compiler_params=pltpu.CompilerParams(

time: 32.4 us -> 31.8 us (0.981)
  Pallas kernels: 32.2 us -> 31.7 us
    pallas_call x1, Pallas kernels: 29.8 us -> 29.3 us  [local(): pl.pallas_call(functools.partial(kernel, counts), out_shape=jax.ShapeDtyp...]
where the time goes in v3:
time: 31.8 us; the launch traced here: 31.7 us
  Pallas kernels  31.7 us (100%)
    pallas_call x1, Pallas kernels, local(): pl.pallas_call(functools.partial(kernel, counts), out_shape=jax.ShapeDtyp...  29.3 us
    pallas_call x1, Pallas kernels, local(): pl.pallas_call(hand_over, out_shape=jax.ShapeDtypeStruct((SX, SY, SZ), F3...  2.42 us

profile of v3, /device:TPU:44, one launch (start us, length us, event | category | flops | bytes accessed | tf_op | source)
XLA Modules:
  0.0 31.7 jit_solution(8611339346492012892)
XLA Ops:
  0.0 29.3 %shard_map.28.src = f32[32,128,128]{2,1,0:T(8,128)} custom-call(s32[4,3]{1,0:T(4,128)} %off.1, f32[32,128,128]{2,1,0:T(8,128)} %v.1), custom_call_target="tpu_custom_call" | custom-call | tf_op jit(solution)/shard_map/pallas_call | solution.py:477
  29.3 2.4 %shard_map.29 = f32[32,128,128]{2,1,0:T(8,128)} custom-call(f32[32,128,128]{2,1,0:T(8,128)} %shard_map.28.src), custom_call_target="tpu_custom_call" | custom-call | tf_op jit(solution)/shard_map/pallas_call | solution.py:518

commit v4 on v3

--- a/solution.py
+++ b/solution.py
@@ -316,7 +316,15 @@
                 eh[k, g, rows, :] = high
                 el[k, g, rows, :] = field - high
 
-    edges([(0, 32)], [(0, 32)], lambda k: [4 + 8 * k + i for i in range(8)])
+    def inner_edges(k):
+        edge_pair(k, [(0, 32)], [(0, 32)])
+
+    def halo_eight(n, _):
+        halo_planes([4 + 8 * n + i for i in range(8)])
+        return 0
+
+    inner_edges(jnp.int32(0))
+    lax.fori_loop(0, 4, halo_eight, 0)
 
 
     def shifts(k):
@@ -388,7 +396,7 @@
                     back = pltpu.roll(jnp.where(beyond, hal[x, at, :], sv[x, at, :]), turn, axis=1)
                     t2[k, p + i + h, rows, :] = back * weight[144 * h + 8 * t : 144 * h + 8 * t + 8, 128:256]
 
-    def run(steps, place):
+    def run(steps, place, beside=None):
         def field(s, xs):
             k, n, slot = place(jnp.minimum(s, steps - 1))
             field_step(k, n, jnp.where(s < steps, slot, 2), xs)
@@ -409,12 +417,14 @@
             weigh(s + 2, xa)
             field(s + 4, xa)
             weigh(s + 3, xb)
+            if beside is not None:
+                beside(i)
             return 0
 
         lax.fori_loop(0, steps // 4, two_steps, 0)
 
     begin(BLOCK, 0)
-    run(PAIRS * 4, lambda s: (s // 4, 1 + s % 4, 0))
+    run(PAIRS * 4, lambda s: (s // 4, 1 + s % 4, 0), lambda i: inner_edges(jnp.minimum(i + 1, PAIRS - 1)))
 
     for item in slabs + ends:
         arrive(item)

time: 31.8 us -> 32.4 us (1.019)
  Pallas kernels: 31.7 us -> 32.1 us
    pallas_call x1, Pallas kernels: 29.3 us -> 29.7 us  [local(): pl.pallas_call(functools.partial(kernel, counts), out_shape=jax.ShapeDtyp...]
where the time goes in v4:
time: 32.4 us; the launch traced here: 32.2 us
  Pallas kernels  32.1 us (99%)
    pallas_call x1, Pallas kernels, local(): pl.pallas_call(functools.partial(kernel, counts), out_shape=jax.ShapeDtyp...  29.7 us
    pallas_call x1, Pallas kernels, local(): pl.pallas_call(hand_over, out_shape=jax.ShapeDtypeStruct((SX, SY, SZ), F3...  2.42 us

profile of v4, /device:TPU:44, one launch (start us, length us, event | category | flops | bytes accessed | tf_op | source)
XLA Modules:
  0.0 32.2 jit_solution(10723561899842876020)
XLA Ops:
  0.0 29.7 %shard_map.28.src = f32[32,128,128]{2,1,0:T(8,128)} custom-call(s32[4,3]{1,0:T(4,128)} %off.1, f32[32,128,128]{2,1,0:T(8,128)} %v.1), custom_call_target="tpu_custom_call" | custom-call | tf_op jit(solution)/shard_map/pallas_call | solution.py:487
  29.7 2.4 %shard_map.29 = f32[32,128,128]{2,1,0:T(8,128)} custom-call(f32[32,128,128]{2,1,0:T(8,128)} %shard_map.28.src), custom_call_target="tpu_custom_call" | custom-call | tf_op jit(solution)/shard_map/pallas_call | solution.py:528
